TPU v7x, 32 devices: a whole 2x2x4 slice. The times are simulated.
32 devices in a mesh: gx: 4 (over x, core), gy: 4 (over z), gz: 2 (over y).
Axes of the slice: x: 2, y: 2, z: 4, core: 2. Of those that a mesh axis runs over, the one named last changes fastest.
Arguments:
- out_grad_values: bfloat16 [256, 28672], P(('gx', 'gy'), 'gz'), may hold values from -6 to 6
- out_grad_scales: bfloat16 [256, 896], P(('gx', 'gy'), 'gz'), may hold values from 0.099609375 to 1
- pre_activation: bfloat16 [256, 28672], P(('gx', 'gy'), 'gz'), may hold values from -8 to 8
- saved_values: bfloat16 [256, 14336], P('gz', ('gx', 'gy')), may hold values from -6 to 6
- saved_scales: bfloat16 [256, 448], P('gz', ('gx', 'gy')), may hold values from 0.19921875 to 2
- up_weight: bfloat16 [14336, 28672], P(('gx', 'gy'), 'gz'), may hold values from -0.046875 to 0.046875
Outputs:
- grad_input: bfloat16 [256, 14336], P('gz', ('gx', 'gy'))
- grad_weight: bfloat16 [14336, 28672], P(('gx', 'gy'), 'gz')
- grad_bias: float32 [28672], P('gz')
All inputs are finite; a program needn't handle non-finite values.
Results may differ from a plain program's by a relative error of at most 0.0059.
Values may be sent and summed in bfloat16 or wider, within the bound.
A program may use at most 192 MiB of HBM per device.

v0:
```python
import jax
import jax.numpy as jnp
from jax import lax
from jax.sharding import PartitionSpec as P


def gelu_slope(preact):
    inner = jnp.tanh(0.79788456 * preact * (1.0 + 0.044715 * preact * preact))
    return 0.5 * preact * (
        (1.0 - inner * inner) * (0.79788456 + 0.1070322243 * preact * preact)
    ) + 0.5 * (1.0 + inner)


def dequantize(values, scales):
    height = values.shape[0]
    blocks = scales.shape[1]
    shaped = (
        values.astype(jnp.float32).reshape(height, blocks, -1)
        * scales.astype(jnp.float32)[:, :, None]
    )
    return shaped.reshape(height, -1)


def slope_product(values, scales, preact):
    return (dequantize(values, scales) * gelu_slope(preact.astype(jnp.float32))).astype(
        jnp.bfloat16
    )


def body(out_grad_values, out_grad_scales, pre_activation, saved_values, saved_scales, up_weight):
    restored = dequantize(saved_values, saved_scales).astype(jnp.bfloat16)
    saved_all = lax.all_gather(restored, "gz", axis=0, tiled=True)
    own_slope = slope_product(out_grad_values, out_grad_scales, pre_activation)
    slope_all = lax.all_gather(own_slope, ("gx", "gy"), axis=0, tiled=True)
    weight_acc = lax.dot_general(
        saved_all, slope_all, (((0,), (0,)), ((), ())), preferred_element_type=jnp.float32
    )
    grad_weight = weight_acc.astype(jnp.bfloat16)
    grad_bias = jnp.sum(slope_all, axis=0, dtype=jnp.float32)
    grad_input = lax.psum_scatter(
        lax.dot_general(
            slope_all, up_weight, (((1,), (1,)), ((), ())), preferred_element_type=jnp.float32
        ).astype(jnp.bfloat16),
        "gz",
        scatter_dimension=0,
        tiled=True,
    )
    return (grad_input, grad_weight, grad_bias)


def solution(mesh):
    placed = (
        P(("gx", "gy"), "gz"),
        P(("gx", "gy"), "gz"),
        P(("gx", "gy"), "gz"),
        P("gz", ("gx", "gy")),
        P("gz", ("gx", "gy")),
        P(("gx", "gy"), "gz"),
    )
    return jax.shard_map(
        body,
        mesh=mesh,
        in_specs=placed,
        out_specs=(P("gz", ("gx", "gy")), P(("gx", "gy"), "gz"), P("gz")),
        check_vma=False,
    )
```

profile of v0, /device:TPU:0, one launch (start us, length us, event | category | flops | bytes accessed | tf_op | source)
XLA Modules:
  0.0 128.9 jit_solution(11815489453578542562)
XLA Ops:
  7.2 0.0 copy-start
  7.2 0.0 copy-start.1
  7.2 0.0 copy-start.2
  7.2 0.0 copy-start.3
  7.2 0.0 all-gather.2.cloned.1.call-start
  7.3 3.2 %mul.64 = f32[16,448,32]{2,1,0:T(8,128)} broadcast(bf16[16,448]{1,0:T(8,128)(2,1)} %param.7), dimensions={0,1} | broadcast | bytes 931840 | tf_op jit(solution)/shard_map/mul | solution.py:18
  10.4 3.2 %mul.65 = f32[16,14336]{1,0:T(8,128)S(1)} reshape(f32[16,448,32]{2,1,0:T(8,128)} %mul.64) | data formatting | bytes 1835008 | tf_op jit(solution)/shard_map/mul | solution.py:18
  13.6 0.0 copy-done
  13.6 0.0 copy-done.1
  13.6 1.4 %fusion.3 = bf16[16,14336]{1,0:T(8,128)(2,1)} fusion(bf16[16,14336]{1,0:T(8,128)(2,1)S(1)} %copy-done, f32[16,14336]{1,0:T(8,128)S(1)} %mul.65, bf16[16,14336]{1,0:T(8,128)(2,1)S(1)} %copy-done.1), kind=kLoop, calls=%fused_computation.12 | loop fusion | flops 4816896 | bytes 2293760 | tf_op jit(solution)/shard_map/convert_element_type | solution.py:25
  15.0 0.0 all-gather.2.cloned.1.call-update
  15.0 0.0 reduce-scatter.2.cloned.1.call-start
  15.1 0.0 copy-done.2
  15.1 0.2 copy.10
  15.3 0.0 copy-done.3
  15.3 0.1 fusion.9
  15.4 9.3 %all_gather.7 = bf16[256,896]{0,1:T(8,128)(2,1)S(1)} all-gather(bf16[128,896]{0,1:T(8,128)(2,1)S(1)} %fusion.9), channel_id=1, replica_groups=mesh['gx'=4,'gy'=4,'gz'=2] {'gz'}, dimensions={0}, use_global_device_ids=true | all-gather | bytes 688128 | tf_op jit(solution)/shard_map/all_gather | solution.py:32
  24.6 61.5 %all-gather.2.cloned.1.call-done = bf16[256,14336]{1,0:T(8,128)(2,1)} async-done(((bf16[16,14336]{1,0:T(8,128)(2,1)}), bf16[256,14336]{1,0:T(8,128)(2,1)}) %all-gather.2.cloned.1.call-update) | async-done | bytes 7340048 | tf_op jit(solution)/shard_map/all_gather | solution.py:34
  86.2 15.2 %convolution_convert_fusion.1 = bf16[256,896]{1,0:T(8,128)(2,1)} fusion(bf16[256,14336]{1,0:T(8,128)(2,1)} %all-gather.2.cloned.1.call-done, bf16[896,14336]{1,0:T(8,128)(2,1)} %param.11), kind=kOutput, calls=%fused_computation.8 | convolution fusion | flops 6576898048 | bytes 33488896 | tf_op jit(solution)/shard_map/dot_general | solution.py:41
  101.4 0.0 reduce-scatter.2.cloned.1.call-update
  101.4 15.7 %convolution_convert_fusion = bf16[896,14336]{1,0:T(8,128)(2,1)} fusion(bf16[256,896]{0,1:T(8,128)(2,1)S(1)} %all_gather.7, bf16[256,14336]{1,0:T(8,128)(2,1)} %all-gather.2.cloned.1.call-done), kind=kOutput, calls=%fused_computation | convolution fusion | flops 6589513728 | bytes 33488896 | tf_op jit(solution)/shard_map/dot_general | solution.py:35
  117.1 4.9 %convert_reduce_fusion = f32[14336]{0:T(1024)} fusion(bf16[256,14336]{1,0:T(8,128)(2,1)} %all-gather.2.cloned.1.call-done), kind=kLoop, calls=%fused_computation.1 | loop fusion | flops 7325696 | bytes 7397376 | tf_op jit(solution)/shard_map/reduce_sum | solution.py:39
  122.1 0.0 reduce-scatter.2.cloned.1.call-done
  (1 shorter events, 0.0 us)
Async XLA Ops:
  7.2 6.4 %copy-start = (bf16[16,14336]{1,0:T(8,128)(2,1)S(1)}, bf16[16,14336]{1,0:T(8,128)(2,1)}, u32[]{:S(2)}) copy-start(bf16[16,14336]{1,0:T(8,128)(2,1)} %param.8) | copy-start | bytes 1376260
  7.2 6.4 %copy-start.1 = (bf16[16,14336]{1,0:T(8,128)(2,1)S(1)}, bf16[16,14336]{1,0:T(8,128)(2,1)}, u32[]{:S(2)}) copy-start(bf16[16,14336]{1,0:T(8,128)(2,1)} %param.6) | copy-start | bytes 1376260
  7.2 7.9 %copy-start.2 = (bf16[128,896]{1,0:T(8,128)(2,1)S(1)}, bf16[128,896]{1,0:T(8,128)(2,1)}, u32[]{:S(2)}) copy-start(bf16[128,896]{1,0:T(8,128)(2,1)} %param.9) | copy-start | bytes 688132
  7.2 8.1 %copy-start.3 = (bf16[128,28]{0,1:T(8,128)(2,1)S(1)}, bf16[128,28]{0,1:T(8,128)(2,1)}, u32[]{:S(2)}) copy-start(bf16[128,28]{0,1:T(8,128)(2,1)} %param.10) | copy-start | bytes 21508
  7.2 79.0 %all-gather.2.cloned.1.call-start = ((), (), s32[]{:S(2)}) async-start(), calls=%async_computation.1 | async-start | bytes 7798784 | tf_op jit(solution)/shard_map/all_gather | solution.py:34
  15.0 107.0 %reduce-scatter.2.cloned.1.call-start = ((), (), s32[]{:S(2)}) async-start(), calls=%async_computation.2 | async-start | bytes 688128 | tf_op jit(solution)/shard_map/reduce_scatter | solution.py:40
Sparse Core Ops, SparseCore 0:
  15.2 70.9 all-gather.1
  101.6 12.2 reduce-scatter.1
where the time goes:
time: 129 us
  waiting for transfers between devices  61.6 us (48%)
  matrix products  31 us (24%)
  between operations  14.1 us (11%)
  blocking collectives  9.27 us (7%)
  local copies, waits for them, and re-layouts  6.52 us (5%)
  other arithmetic  6.39 us (5%)
    all_gather x1, waiting for transfers between devices, body(): slope_all = lax.all_gather(own_slope, ('gx', 'gy'), axis=0, tiled=True)  61.5 us
    dot_general x1, matrix products, body(): lax.dot_general(saved_all, slope_all, (((0,), (0,)), ((), ())), preferred...  15.7 us
    dot_general x1, matrix products, body(): lax.dot_general(slope_all, up_weight, (((1,), (1,)), ((), ())), preferred...  15.2 us
    all_gather x1, blocking collectives, body(): saved_all = lax.all_gather(restored, 'gz', axis=0, tiled=True)  9.27 us
    mul x2, local copies, waits for them, and re-layouts, dequantize(): values.astype(jnp.float32).reshape(height, blocks, -1)  6.33 us
    reduce_sum x1, other arithmetic, body(): grad_bias = jnp.sum(slope_all, axis=0, dtype=jnp.float32)  4.92 us
  transfers between devices with their start and end apart: 2, of which 1 were waited for; matrix products, arithmetic and copies ran while one was open for 16% of the time, Pallas kernels for 0%

commit v1 on v0

--- a/solution.py
+++ b/solution.py
@@ -1,7 +1,14 @@
+import functools
 import jax
 import jax.numpy as jnp
 from jax import lax
+from jax.experimental import pallas as pl
+from jax.experimental.pallas import tpu as pltpu
 from jax.sharding import PartitionSpec as P
+
+MESH = pl.DeviceIdType.MESH
+WIDTH = 1024
+SPAN = 4096
 
 
 def gelu_slope(preact):
@@ -27,7 +34,7 @@
     )
 
 
-def body(out_grad_values, out_grad_scales, pre_activation, saved_values, saved_scales, up_weight):
+def plain_body(out_grad_values, out_grad_scales, pre_activation, saved_values, saved_scales, up_weight):
     restored = dequantize(saved_values, saved_scales).astype(jnp.bfloat16)
     saved_all = lax.all_gather(restored, "gz", axis=0, tiled=True)
     own_slope = slope_product(out_grad_values, out_grad_scales, pre_activation)
@@ -48,6 +55,268 @@
     return (grad_input, grad_weight, grad_bias)
 
 
+def gather_kernel(
+    nz, values, scales, preact, saved, saved_scales, weight,
+    keep, give, bias, saved_t, hid_out,
+    hid, wbuf, spread, padded, saved_all, acc,
+    w_sem, out_sem, y_send, y_recv,
+    right_send, left_send, x_send, sib_send, z_recv, x_recv, sib_recv,
+):
+    rows = values.shape[0]
+    chunks = hid.shape[0]
+    width = hid.shape[2]
+    per = SPAN // width
+    column = nz * rows
+    gx, z, y = lax.axis_index("gx"), lax.axis_index("gy"), lax.axis_index("gz")
+    x, c = gx // 2, gx % 2
+    partner_gx, sib_gx = (1 - x) * 2 + c, x * 2 + 1 - c
+
+    to_right = {"gy": jnp.minimum(z + 1, nz - 1)}
+    to_left = {"gy": jnp.maximum(z - 1, 0)}
+    to_x, to_sib, to_y = {"gx": partner_gx}, {"gx": sib_gx}, {"gz": 1 - y}
+
+    def block(k, gx_at, z_at):
+        at = pl.multiple_of((gx_at * nz + z_at) * rows, rows)
+        return hid.at[k, pl.ds(at, rows), :]
+
+    def block_column(k, gx_at):
+        return hid.at[k, pl.ds(pl.multiple_of(gx_at * column, column), column), :]
+
+    def landed(ref, sem):
+        pltpu.make_async_copy(ref, ref, sem).wait()
+
+    def send(ref, s_sem, r_sem, to):
+        pltpu.make_async_remote_copy(
+            src_ref=ref, dst_ref=ref, send_sem=s_sem, recv_sem=r_sem,
+            device_id=to, device_id_type=MESH,
+        ).start()
+
+    def w_copy(k):
+        return pltpu.make_async_copy(
+            weight.at[:, pl.ds(pl.multiple_of(k * width, width), width)],
+            wbuf.at[k], w_sem.at[k],
+        )
+
+    barrier = pltpu.get_barrier_semaphore()
+
+    @pl.when(z + 1 < nz)
+    def _():
+        pl.semaphore_signal(barrier, inc=1, device_id=to_right, device_id_type=MESH)
+
+    @pl.when(z > 0)
+    def _():
+        pl.semaphore_signal(barrier, inc=1, device_id=to_left, device_id_type=MESH)
+
+    for to in (to_x, to_sib, to_y):
+        pl.semaphore_signal(barrier, inc=1, device_id=to, device_id_type=MESH)
+
+    def fetch(k, carry):
+        w_copy(k).start()
+        return carry
+
+    lax.fori_loop(0, chunks, fetch, 0)
+
+    shape = (128, SPAN)
+    spread[...] = (
+        lax.broadcasted_iota(jnp.int32, shape, 0)
+        == lax.broadcasted_iota(jnp.int32, shape, 1) // 32
+    ).astype(jnp.float32).astype(jnp.bfloat16)
+    padded[...] = jnp.zeros_like(padded)
+    padded[:, : scales.shape[1]] = scales[...]
+    acc[...] = jnp.zeros_like(acc)
+
+    middle = jnp.where(z > 0, 1, 0) + jnp.where(z + 1 < nz, 1, 0)
+    pl.semaphore_wait(barrier, 3 + middle)
+
+    def own(k):
+        cols = pl.ds(pl.multiple_of(k * width, width), width)
+        scale = jnp.dot(
+            padded[:, pl.ds(pl.multiple_of(k // per * 128, 128), 128)],
+            spread[:, pl.ds(pl.multiple_of(k % per * width, width), width)],
+            preferred_element_type=jnp.float32,
+        )
+        gradient = values[:, cols].astype(jnp.float32) * scale
+        result = gradient * gelu_slope(preact[:, cols].astype(jnp.float32))
+        at = pl.multiple_of((gx * nz + z) * rows, rows)
+        hid[k, pl.ds(at, rows), :] = result.astype(jnp.bfloat16)
+        forward(k, z, 0, True, True)
+
+    def forward(k, z_at, hop, rightward, leftward):
+        ref = block(k, gx, z_at)
+        if hop < nz - 1:
+            if rightward:
+                @pl.when(z + 1 < nz)
+                def _():
+                    send(ref, right_send.at[hop], z_recv.at[k, z_at], to_right)
+            if leftward:
+                @pl.when(z > 0)
+                def _():
+                    send(ref, left_send.at[hop], z_recv.at[k, z_at], to_left)
+        send(ref, x_send, x_recv.at[k], to_x)
+
+    def arrived(k, hop):
+        @pl.when(z >= hop)
+        def _():
+            landed(block(k, gx, z - hop), z_recv.at[k, z - hop])
+            forward(k, z - hop, hop, True, False)
+
+        @pl.when(z + hop < nz)
+        def _():
+            landed(block(k, gx, z + hop), z_recv.at[k, z + hop])
+            forward(k, z + hop, hop, False, True)
+
+    def from_x(k):
+        ref = block_column(k, partner_gx)
+        landed(ref, x_recv.at[k])
+        send(ref, sib_send, sib_recv.at[k, 1], to_sib)
+
+    def use(k):
+        landed(block_column(k, sib_gx), sib_recv.at[k, 0])
+        landed(block_column(k, (1 - x) * 2 + 1 - c), sib_recv.at[k, 1])
+        pltpu.make_async_copy(hid.at[k], hid_out.at[k], out_sem).start()
+        w_copy(k).wait()
+        acc[...] += lax.dot_general(
+            hid[k], wbuf[k], (((1,), (1,)), ((), ())), preferred_element_type=jnp.float32
+        )
+        cols = pl.ds(pl.multiple_of(k * width, width), width)
+        bias[:, cols] = jnp.sum(hid[k].astype(jnp.float32), axis=0, keepdims=True)
+
+    def within(k, fn):
+        @pl.when((k >= 0) & (k < chunks))
+        def _():
+            fn(k)
+
+    def step(t, carry):
+        within(t, own)
+        for hop in range(1, nz):
+            within(t - hop, functools.partial(arrived, hop=hop))
+        within(
+            t - (nz - 1),
+            lambda k: send(block_column(k, gx), sib_send, sib_recv.at[k, 0], to_sib),
+        )
+        within(t - nz, from_x)
+        within(t - nz - 1, use)
+        return carry
+
+    own(0)
+    half = saved.shape[0]
+    wide = saved.shape[1]
+    acc[0:half, 0:128] = jnp.zeros((half, 128), jnp.float32)
+    acc[0:half, 0 : saved_scales.shape[1]] = saved_scales[...].astype(jnp.float32)
+    restored = (
+        jnp.dot(
+            acc[0:half, 0:128].astype(jnp.bfloat16), spread[:, :wide],
+            preferred_element_type=jnp.float32,
+        )
+        * saved[...].astype(jnp.float32)
+    ).astype(jnp.bfloat16)
+    acc[0:half, 0:128] = jnp.zeros((half, 128), jnp.float32)
+    own_half = pl.ds(pl.multiple_of(y * half, half), half)
+    other_half = pl.ds(pl.multiple_of((1 - y) * half, half), half)
+    saved_all[own_half, :] = restored
+    send(saved_all.at[own_half, :], y_send, y_recv, to_y)
+
+    lax.fori_loop(1, nz, step, 0)
+    lax.fori_loop(nz, chunks, step, 0)
+    landed(saved_all.at[other_half, :], y_recv)
+    saved_t[...] = saved_all[...].T
+    lax.fori_loop(chunks, chunks + nz + 1, step, 0)
+
+    keep[...] = acc[own_half, :].astype(jnp.bfloat16)
+    give[...] = acc[other_half, :].astype(jnp.bfloat16)
+
+    landed(saved_all.at[own_half, :], y_send)
+    for hop in range(nz - 1):
+        @pl.when((z + 1 < nz) & (z >= hop))
+        def _():
+            landed(hid.at[:, 0:rows, :], right_send.at[hop])
+
+        @pl.when((z > 0) & (z + hop < nz))
+        def _():
+            landed(hid.at[:, 0:rows, :], left_send.at[hop])
+
+    landed(hid.at[:, 0:column, :], x_send)
+    landed(hid.at[:, 0 : 2 * column, :], sib_send)
+    pltpu.make_async_copy(hid, hid_out, out_sem).wait()
+
+
+def weight_kernel(saved_t, hid, bias, out, bias_out):
+    out[...] = jnp.dot(
+        saved_t[...], hid[0], preferred_element_type=jnp.float32
+    ).astype(out.dtype)
+    bias_out[...] = bias[...]
+
+
+def fast_body(nz, values, scales, preact, saved, saved_scales, weight):
+    rows, hidden = values.shape
+    wide = weight.shape[0]
+    half = saved.shape[0]
+    tokens = 4 * nz * rows
+    chunks = hidden // WIDTH
+    vmem = pl.BlockSpec(memory_space=pltpu.VMEM)
+    hbm = pl.BlockSpec(memory_space=pltpu.HBM)
+    dma = pltpu.SemaphoreType.DMA
+    keep, give, bias, saved_t, hid = pl.pallas_call(
+        functools.partial(gather_kernel, nz),
+        out_shape=(
+            jax.ShapeDtypeStruct((half, wide), jnp.bfloat16),
+            jax.ShapeDtypeStruct((half, wide), jnp.bfloat16),
+            jax.ShapeDtypeStruct((1, hidden), jnp.float32),
+            jax.ShapeDtypeStruct((wide, tokens), jnp.bfloat16),
+            jax.ShapeDtypeStruct((chunks, tokens, WIDTH), jnp.bfloat16),
+        ),
+        in_specs=[vmem] * 5 + [hbm],
+        out_specs=(vmem, vmem, vmem, vmem, hbm),
+        scratch_shapes=[
+            pltpu.VMEM((chunks, tokens, WIDTH), jnp.bfloat16),
+            pltpu.VMEM((chunks, wide, WIDTH), jnp.bfloat16),
+            pltpu.VMEM((128, SPAN), jnp.bfloat16),
+            pltpu.VMEM((rows, pl.cdiv(scales.shape[1], 128) * 128), jnp.bfloat16),
+            pltpu.VMEM((tokens, wide), jnp.bfloat16),
+            pltpu.VMEM((tokens, wide), jnp.float32),
+            dma((chunks,)), dma, dma, dma,
+            dma((nz - 1,)), dma((nz - 1,)), dma, dma,
+            dma((chunks, nz)), dma((chunks,)), dma((chunks, 2)),
+        ],
+        compiler_params=pltpu.CompilerParams(
+            collective_id=0, has_side_effects=True, vmem_limit_bytes=52 << 20
+        ),
+        cost_estimate=pl.CostEstimate(
+            flops=2 * tokens * hidden * wide,
+            bytes_accessed=2 * hidden * (wide + tokens),
+            transcendentals=rows * hidden,
+        ),
+        name="gather",
+    )(values, scales, preact, saved, saved_scales, weight)
+    taken = lax.ppermute(give, "gz", [(0, 1), (1, 0)])
+    grad_weight, grad_bias = pl.pallas_call(
+        weight_kernel,
+        grid=(chunks,),
+        out_shape=(
+            jax.ShapeDtypeStruct((wide, hidden), jnp.bfloat16),
+            jax.ShapeDtypeStruct((1, hidden), jnp.float32),
+        ),
+        in_specs=[
+            pl.BlockSpec((wide, tokens), lambda i: (0, 0)),
+            pl.BlockSpec((1, tokens, WIDTH), lambda i: (i, 0, 0)),
+            pl.BlockSpec((1, WIDTH), lambda i: (0, i)),
+        ],
+        out_specs=(
+            pl.BlockSpec((wide, WIDTH), lambda i: (0, i)),
+            pl.BlockSpec((1, WIDTH), lambda i: (0, i)),
+        ),
+        compiler_params=pltpu.CompilerParams(vmem_limit_bytes=32 << 20),
+        cost_estimate=pl.CostEstimate(
+            flops=2 * tokens * hidden * wide,
+            bytes_accessed=2 * hidden * (wide + tokens),
+            transcendentals=0,
+        ),
+        name="weight",
+    )(saved_t, hid, bias)
+    grad_input = (keep.astype(jnp.float32) + taken.astype(jnp.float32)).astype(jnp.bfloat16)
+    return grad_input, grad_weight, grad_bias.reshape(-1)
+
+
 def solution(mesh):
     placed = (
         P(("gx", "gy"), "gz"),
@@ -57,6 +326,9 @@
         P("gz", ("gx", "gy")),
         P(("gx", "gy"), "gz"),
     )
+    body = plain_body
+    if mesh.shape["gx"] == 4 and mesh.shape["gz"] == 2:
+        body = functools.partial(fast_body, mesh.shape["gy"])
     return jax.shard_map(
         body,
         mesh=mesh,

time: 129 us -> 79.5 us (0.62)
  Pallas kernels: 0 us -> 70 us
  waiting for transfers between devices: 61.6 us -> 0.01 us
  matrix products: 31 us -> 0 us
  between operations: 14.1 us -> 0.64 us
  blocking collectives: 9.27 us -> 0 us
  other arithmetic: 6.39 us -> 0.74 us
    pallas_call x0 -> x2, Pallas kernels: none -> 70 us  [the longest x1 56.2 us: fast_body(): pl.pallas_call(functools.partial(gather_kernel, nz), out_shape=(jax.Shape...]
    all_gather x1 -> x0, waiting for transfers between devices: 61.5 us -> none  [body(): slope_all = lax.all_gather(own_slope, ('gx', 'gy'), axis=0, tiled=True)]
    dot_general x2 -> x0, matrix products: 31 us -> none  [the longest x1 15.7 us: body(): lax.dot_general(saved_all, slope_all, (((0,), (0,)), ((), ())), preferred...]
    all_gather x1 -> x0, blocking collectives: 9.27 us -> none  [body(): saved_all = lax.all_gather(restored, 'gz', axis=0, tiled=True)]
    unnamed x9, local copies, waits for them, and re-layouts: 0.19 us -> 6.58 us
    mul x2 -> x0, local copies, waits for them, and re-layouts: 6.33 us -> none  [dequantize(): values.astype(jnp.float32).reshape(height, blocks, -1)]
    reduce_sum x1 -> x0, other arithmetic: 4.92 us -> none  [body(): grad_bias = jnp.sum(slope_all, axis=0, dtype=jnp.float32)]
  transfers between devices with their start and end apart: 2 -> 1, of which waited for: 1 -> 0; matrix products, arithmetic and copies ran while one was open for 16% -> 0% of each run, Pallas kernels for 0% -> 17%
where the time goes in v1:
time: 79.5 us; the launch traced here: 79.1 us
  Pallas kernels  70 us (88%)
  local copies, waits for them, and re-layouts  6.58 us (8%)
  starting transfers between devices  1.18 us (1%)
    pallas_call x1, Pallas kernels, fast_body(): pl.pallas_call(functools.partial(gather_kernel, nz), out_shape=(jax.Shape...  56.2 us
    pallas_call x1, Pallas kernels, fast_body(): pl.pallas_call(weight_kernel, grid=(chunks,), out_shape=(jax.ShapeDtypeSt...  13.8 us
    unnamed x9, local copies, waits for them, and re-layouts  6.58 us
  transfers between devices with their start and end apart: 1, of which 0 were waited for; matrix products, arithmetic and copies ran while one was open for 0% of the time, Pallas kernels for 17%

profile of v1, /device:TPU:0, one launch (start us, length us, event | category | flops | bytes accessed | tf_op | source)
XLA Modules:
  0.0 79.1 jit_solution(15847162284753245913)
XLA Ops:
  0.6 0.8 %copy.9.saved_scales = bf16[128,28]{1,0:T(8,128)(2,1)S(1)} copy(bf16[128,28]{0,1:T(8,128)(2,1)} %param.10) | data formatting | bytes 14336 | tf_op args[4]
  1.4 0.0 copy-start
  1.5 1.0 %copy-done = bf16[16,14336]{1,0:T(8,128)(2,1)S(1)} copy-done((bf16[16,14336]{1,0:T(8,128)(2,1)S(1)}, bf16[16,14336]{1,0:T(8,128)(2,1)}, u32[]{:S(2)}) %copy-start) | copy-done | bytes 458776
  2.5 0.0 copy-start.1
  2.5 0.9 %copy-done.1 = bf16[128,896]{1,0:T(8,128)(2,1)S(1)} copy-done((bf16[128,896]{1,0:T(8,128)(2,1)S(1)}, bf16[128,896]{1,0:T(8,128)(2,1)}, u32[]{:S(2)}) %copy-start.1) | copy-done | bytes 229400
  3.4 0.0 copy-start.2
  3.4 0.7 copy-done.2
  4.1 56.2 %gather.1 = (bf16[128,896]{1,0:T(8,128)(2,1)S(1)}, bf16[128,896]{1,0:T(8,128)(2,1)S(1)}, f32[1,14336]{1,0:T(1,128)S(1)}, bf16[896,256]{1,0:T(8,128)(2,1)S(1)}, bf16[14,256,1024]{2,1,0:T(8,128)(2,1)}) custom-call(bf16[16,14336]{1,0:T(8,128)(2,1)S(1)} %copy-done, bf16[16,448]{1,0:T(8,128)(2,1)S(1)} %copy-done.2, bf16[16,14336]{1,0:T(8,128)(2,1)} %preact.1, ...), custom_call_target="tpu_custom_call" | custom-call | flops 6576668672 | bytes 33030144 | tf_op jit(solution)/shard_map/gather/pallas_call | solution.py:259
  60.3 1.2 %collective-permute-start = (bf16[128,896]{1,0:T(8,128)(2,1)S(1)}, bf16[128,896]{1,0:T(8,128)(2,1)S(1)}, u32[]{:S(2)}, u32[]{:S(2)}) collective-permute-start(bf16[128,896]{1,0:T(8,128)(2,1)S(1)} %get-tuple-element.11), channel_id=1, source_target_pairs={{0,1},{1,0},{2,3},{3,2},{4,5},{5,4},{6,7},{7,6},{8,9},{9,8},{10,11... | collective-permute-start | bytes 688136 | tf_op jit(solution)/shard_map/ppermute | solution.py:291
  61.5 0.0 copy-start.3
  61.5 3.1 %copy-done.3 = bf16[14,256,1024]{2,1,0:T(8,128)(2,1)S(1)} copy-done((bf16[14,256,1024]{2,1,0:T(8,128)(2,1)S(1)}, bf16[14,256,1024]{2,1,0:T(8,128)(2,1)}, u32[]{:S(2)}) %copy-start.3) | copy-done | bytes 7340056
  64.6 13.8 %weight.3 = (bf16[896,14336]{1,0:T(8,128)(2,1)}, f32[1,14336]{1,0:T(1,128)}) custom-call(bf16[896,256]{1,0:T(8,128)(2,1)S(1)} %get-tuple-element.12.saved_t, bf16[14,256,1024]{2,1,0:T(8,128)(2,1)S(1)} %copy-done.3, f32[1,14336]{1,0:T(1,128)S(1)} %get-tuple-element.14.bias), custom_call_target="tpu_custom_call" | custom-call | flops 6576668672 | bytes 33030144 | tf_op jit(solution)/shard_map/weight/pallas_call | solution.py:292
  78.4 0.0 collective-permute-done
  78.4 0.7 add_convert_fusion
Async XLA Ops:
  1.4 1.0 %copy-start = (bf16[16,14336]{1,0:T(8,128)(2,1)S(1)}, bf16[16,14336]{1,0:T(8,128)(2,1)}, u32[]{:S(2)}) copy-start(bf16[16,14336]{1,0:T(8,128)(2,1)} %values.1) | copy-start | bytes 1376260
  2.5 0.9 %copy-start.1 = (bf16[128,896]{1,0:T(8,128)(2,1)S(1)}, bf16[128,896]{1,0:T(8,128)(2,1)}, u32[]{:S(2)}) copy-start(bf16[128,896]{1,0:T(8,128)(2,1)} %saved.1) | copy-start | bytes 688132
  3.4 0.7 copy-start.2
  60.3 18.0 %collective-permute-start = (bf16[128,896]{1,0:T(8,128)(2,1)S(1)}, bf16[128,896]{1,0:T(8,128)(2,1)S(1)}, u32[]{:S(2)}, u32[]{:S(2)}) collective-permute-start(bf16[128,896]{1,0:T(8,128)(2,1)S(1)} %get-tuple-element.11), channel_id=1, source_target_pairs={{0,1},{1,0},{2,3},{3,2},{4,5},{5,4},{6,7},{7,6},{8,9},{9,8},{10,11... | collective-permute-start | bytes 688136 | tf_op jit(solution)/shard_map/ppermute | solution.py:291
  61.5 3.1 %copy-start.3 = (bf16[14,256,1024]{2,1,0:T(8,128)(2,1)S(1)}, bf16[14,256,1024]{2,1,0:T(8,128)(2,1)}, u32[]{:S(2)}) copy-start(bf16[14,256,1024]{2,1,0:T(8,128)(2,1)} %get-tuple-element.13.hid) | copy-start | bytes 22020100

commit v2 on v1

--- a/solution.py
+++ b/solution.py
@@ -8,6 +8,7 @@
 
 MESH = pl.DeviceIdType.MESH
 WIDTH = 1024
+PAIR = 2
 SPAN = 4096
 
 
@@ -241,9 +242,10 @@
 
 
 def weight_kernel(saved_t, hid, bias, out, bias_out):
-    out[...] = jnp.dot(
-        saved_t[...], hid[0], preferred_element_type=jnp.float32
-    ).astype(out.dtype)
+    for i in range(PAIR):
+        out[:, i * WIDTH : (i + 1) * WIDTH] = jnp.dot(
+            saved_t[...], hid[i], preferred_element_type=jnp.float32
+        ).astype(out.dtype)
     bias_out[...] = bias[...]
 
 
@@ -291,19 +293,19 @@
     taken = lax.ppermute(give, "gz", [(0, 1), (1, 0)])
     grad_weight, grad_bias = pl.pallas_call(
         weight_kernel,
-        grid=(chunks,),
+        grid=(chunks // PAIR,),
         out_shape=(
             jax.ShapeDtypeStruct((wide, hidden), jnp.bfloat16),
             jax.ShapeDtypeStruct((1, hidden), jnp.float32),
         ),
         in_specs=[
             pl.BlockSpec((wide, tokens), lambda i: (0, 0)),
-            pl.BlockSpec((1, tokens, WIDTH), lambda i: (i, 0, 0)),
-            pl.BlockSpec((1, WIDTH), lambda i: (0, i)),
+            pl.BlockSpec((PAIR, tokens, WIDTH), lambda i: (i, 0, 0)),
+            pl.BlockSpec((1, PAIR * WIDTH), lambda i: (0, i)),
         ],
         out_specs=(
-            pl.BlockSpec((wide, WIDTH), lambda i: (0, i)),
-            pl.BlockSpec((1, WIDTH), lambda i: (0, i)),
+            pl.BlockSpec((wide, PAIR * WIDTH), lambda i: (0, i)),
+            pl.BlockSpec((1, PAIR * WIDTH), lambda i: (0, i)),
         ),
         compiler_params=pltpu.CompilerParams(vmem_limit_bytes=32 << 20),
         cost_estimate=pl.CostEstimate(

time: 79.5 us -> 77.5 us (0.975)
  Pallas kernels: 70 us -> 68 us
    pallas_call x1, Pallas kernels: 13.8 us -> 11.8 us  [fast_body(): pl.pallas_call(weight_kernel, grid=(chunks // PAIR,), out_shape=(jax.Shap...]
  transfers between devices with their start and end apart: 1 -> 1, of which waited for: 0 -> 0; matrix products, arithmetic and copies ran while one was open for 0% -> 0% of each run, Pallas kernels for 17% -> 15%
where the time goes in v2:
time: 77.5 us; the launch traced here: 77.2 us
  Pallas kernels  68 us (88%)
  local copies, waits for them, and re-layouts  6.58 us (8%)
  starting transfers between devices  1.18 us (2%)
    pallas_call x1, Pallas kernels, fast_body(): pl.pallas_call(functools.partial(gather_kernel, nz), out_shape=(jax.Shape...  56.2 us
    pallas_call x1, Pallas kernels, fast_body(): pl.pallas_call(weight_kernel, grid=(chunks // PAIR,), out_shape=(jax.Shap...  11.8 us
    unnamed x9, local copies, waits for them, and re-layouts  6.58 us
  transfers between devices with their start and end apart: 1, of which 0 were waited for; matrix products, arithmetic and copies ran while one was open for 0% of the time, Pallas kernels for 15%

profile of v2, /device:TPU:0, one launch (start us, length us, event | category | flops | bytes accessed | tf_op | source)
XLA Modules:
  0.0 77.2 jit_solution(16996852813194811624)
XLA Ops:
  0.6 0.8 %copy.9.saved_scales = bf16[128,28]{1,0:T(8,128)(2,1)S(1)} copy(bf16[128,28]{0,1:T(8,128)(2,1)} %param.10) | data formatting | bytes 14336 | tf_op args[4]
  1.4 0.0 copy-start
  1.5 1.0 %copy-done = bf16[16,14336]{1,0:T(8,128)(2,1)S(1)} copy-done((bf16[16,14336]{1,0:T(8,128)(2,1)S(1)}, bf16[16,14336]{1,0:T(8,128)(2,1)}, u32[]{:S(2)}) %copy-start) | copy-done | bytes 458776
  2.5 0.0 copy-start.1
  2.5 0.9 %copy-done.1 = bf16[128,896]{1,0:T(8,128)(2,1)S(1)} copy-done((bf16[128,896]{1,0:T(8,128)(2,1)S(1)}, bf16[128,896]{1,0:T(8,128)(2,1)}, u32[]{:S(2)}) %copy-start.1) | copy-done | bytes 229400
  3.4 0.0 copy-start.2
  3.4 0.7 copy-done.2
  4.1 56.2 %gather.1 = (bf16[128,896]{1,0:T(8,128)(2,1)S(1)}, bf16[128,896]{1,0:T(8,128)(2,1)S(1)}, f32[1,14336]{1,0:T(1,128)S(1)}, bf16[896,256]{1,0:T(8,128)(2,1)S(1)}, bf16[14,256,1024]{2,1,0:T(8,128)(2,1)}) custom-call(bf16[16,14336]{1,0:T(8,128)(2,1)S(1)} %copy-done, bf16[16,448]{1,0:T(8,128)(2,1)S(1)} %copy-done.2, bf16[16,14336]{1,0:T(8,128)(2,1)} %preact.1, ...), custom_call_target="tpu_custom_call" | custom-call | flops 6576668672 | bytes 33030144 | tf_op jit(solution)/shard_map/gather/pallas_call | solution.py:261
  60.3 1.2 %collective-permute-start = (bf16[128,896]{1,0:T(8,128)(2,1)S(1)}, bf16[128,896]{1,0:T(8,128)(2,1)S(1)}, u32[]{:S(2)}, u32[]{:S(2)}) collective-permute-start(bf16[128,896]{1,0:T(8,128)(2,1)S(1)} %get-tuple-element.11), channel_id=1, source_target_pairs={{0,1},{1,0},{2,3},{3,2},{4,5},{5,4},{6,7},{7,6},{8,9},{9,8},{10,11... | collective-permute-start | bytes 688136 | tf_op jit(solution)/shard_map/ppermute | solution.py:293
  61.5 0.0 copy-start.3
  61.5 3.1 %copy-done.3 = bf16[14,256,1024]{2,1,0:T(8,128)(2,1)S(1)} copy-done((bf16[14,256,1024]{2,1,0:T(8,128)(2,1)S(1)}, bf16[14,256,1024]{2,1,0:T(8,128)(2,1)}, u32[]{:S(2)}) %copy-start.3) | copy-done | bytes 7340056
  64.6 11.8 %weight.3 = (bf16[896,14336]{1,0:T(8,128)(2,1)}, f32[1,14336]{1,0:T(1,128)}) custom-call(bf16[896,256]{1,0:T(8,128)(2,1)S(1)} %get-tuple-element.12.saved_t, bf16[14,256,1024]{2,1,0:T(8,128)(2,1)S(1)} %copy-done.3, f32[1,14336]{1,0:T(1,128)S(1)} %get-tuple-element.14.bias), custom_call_target="tpu_custom_call" | custom-call | flops 6576668672 | bytes 33030144 | tf_op jit(solution)/shard_map/weight/pallas_call | solution.py:294
  76.4 0.0 collective-permute-done
  76.4 0.7 add_convert_fusion
Async XLA Ops:
  1.4 1.0 %copy-start = (bf16[16,14336]{1,0:T(8,128)(2,1)S(1)}, bf16[16,14336]{1,0:T(8,128)(2,1)}, u32[]{:S(2)}) copy-start(bf16[16,14336]{1,0:T(8,128)(2,1)} %values.1) | copy-start | bytes 1376260
  2.5 0.9 %copy-start.1 = (bf16[128,896]{1,0:T(8,128)(2,1)S(1)}, bf16[128,896]{1,0:T(8,128)(2,1)}, u32[]{:S(2)}) copy-start(bf16[128,896]{1,0:T(8,128)(2,1)} %saved.1) | copy-start | bytes 688132
  3.4 0.7 copy-start.2
  60.3 16.1 %collective-permute-start = (bf16[128,896]{1,0:T(8,128)(2,1)S(1)}, bf16[128,896]{1,0:T(8,128)(2,1)S(1)}, u32[]{:S(2)}, u32[]{:S(2)}) collective-permute-start(bf16[128,896]{1,0:T(8,128)(2,1)S(1)} %get-tuple-element.11), channel_id=1, source_target_pairs={{0,1},{1,0},{2,3},{3,2},{4,5},{5,4},{6,7},{7,6},{8,9},{9,8},{10,11... | collective-permute-start | bytes 688136 | tf_op jit(solution)/shard_map/ppermute | solution.py:293
  61.5 3.1 %copy-start.3 = (bf16[14,256,1024]{2,1,0:T(8,128)(2,1)S(1)}, bf16[14,256,1024]{2,1,0:T(8,128)(2,1)}, u32[]{:S(2)}) copy-start(bf16[14,256,1024]{2,1,0:T(8,128)(2,1)} %get-tuple-element.13.hid) | copy-start | bytes 22020100

commit v3 on v2

--- a/solution.py
+++ b/solution.py
@@ -7,8 +7,8 @@
 from jax.sharding import PartitionSpec as P
 
 MESH = pl.DeviceIdType.MESH
-WIDTH = 1024
-PAIR = 2
+WIDTH = 2048
+PAIR = 1
 SPAN = 4096
 
 

time: 77.5 us -> 73 us (0.942)
  Pallas kernels: 68 us -> 63 us
    pallas_call x1, Pallas kernels: 56.2 us -> 51.1 us  [fast_body(): pl.pallas_call(functools.partial(gather_kernel, nz), out_shape=(jax.Shape...]
  transfers between devices with their start and end apart: 1 -> 1, of which waited for: 0 -> 0; matrix products, arithmetic and copies ran while one was open for 0% -> 0% of each run, Pallas kernels for 15% -> 16%
where the time goes in v3:
time: 73 us; the launch traced here: 72.6 us
  Pallas kernels  63 us (86%)
  local copies, waits for them, and re-layouts  6.58 us (9%)
  starting transfers between devices  1.71 us (2%)
  other arithmetic  0.74 us (1%)
    pallas_call x1, Pallas kernels, fast_body(): pl.pallas_call(functools.partial(gather_kernel, nz), out_shape=(jax.Shape...  51.1 us
    pallas_call x1, Pallas kernels, fast_body(): pl.pallas_call(weight_kernel, grid=(chunks // PAIR,), out_shape=(jax.Shap...  11.8 us
    unnamed x9, local copies, waits for them, and re-layouts  6.58 us
    ppermute x1, starting transfers between devices, fast_body(): taken = lax.ppermute(give, 'gz', [(0, 1), (1, 0)])  1.71 us
  transfers between devices with their start and end apart: 1, of which 0 were waited for; matrix products, arithmetic and copies ran while one was open for 0% of the time, Pallas kernels for 16%

profile of v3, /device:TPU:0, one launch (start us, length us, event | category | flops | bytes accessed | tf_op | source)
XLA Modules:
  0.0 72.6 jit_solution(211813108240497929)
XLA Ops:
  0.6 0.8 %copy.9.saved_scales = bf16[128,28]{1,0:T(8,128)(2,1)S(1)} copy(bf16[128,28]{0,1:T(8,128)(2,1)} %param.10) | data formatting | bytes 14336 | tf_op args[4]
  1.4 0.0 copy-start
  1.5 1.0 %copy-done = bf16[16,14336]{1,0:T(8,128)(2,1)S(1)} copy-done((bf16[16,14336]{1,0:T(8,128)(2,1)S(1)}, bf16[16,14336]{1,0:T(8,128)(2,1)}, u32[]{:S(2)}) %copy-start) | copy-done | bytes 458776
  2.5 0.0 copy-start.1
  2.5 0.9 %copy-done.1 = bf16[128,896]{1,0:T(8,128)(2,1)S(1)} copy-done((bf16[128,896]{1,0:T(8,128)(2,1)S(1)}, bf16[128,896]{1,0:T(8,128)(2,1)}, u32[]{:S(2)}) %copy-start.1) | copy-done | bytes 229400
  3.4 0.0 copy-start.2
  3.4 0.7 copy-done.2
  4.1 51.1 %gather.1 = (bf16[128,896]{1,0:T(8,128)(2,1)S(1)}, bf16[128,896]{1,0:T(8,128)(2,1)S(1)}, f32[1,14336]{1,0:T(1,128)S(1)}, bf16[896,256]{1,0:T(8,128)(2,1)S(1)}, bf16[7,256,2048]{2,1,0:T(8,128)(2,1)}) custom-call(bf16[16,14336]{1,0:T(8,128)(2,1)S(1)} %copy-done, bf16[16,448]{1,0:T(8,128)(2,1)S(1)} %copy-done.2, bf16[16,14336]{1,0:T(8,128)(2,1)} %preact.1, ...), custom_call_target="tpu_custom_call" | custom-call | flops 6576668672 | bytes 33030144 | tf_op jit(solution)/shard_map/gather/pallas_call | solution.py:261
  55.3 1.7 %collective-permute-start = (bf16[128,896]{1,0:T(8,128)(2,1)S(1)}, bf16[128,896]{1,0:T(8,128)(2,1)S(1)}, u32[]{:S(2)}, u32[]{:S(2)}) collective-permute-start(bf16[128,896]{1,0:T(8,128)(2,1)S(1)} %get-tuple-element.11), channel_id=1, source_target_pairs={{0,1},{1,0},{2,3},{3,2},{4,5},{5,4},{6,7},{7,6},{8,9},{9,8},{10,11... | collective-permute-start | bytes 688136 | tf_op jit(solution)/shard_map/ppermute | solution.py:293
  57.0 0.0 copy-start.3
  57.0 3.1 %copy-done.3 = bf16[7,256,2048]{2,1,0:T(8,128)(2,1)S(1)} copy-done((bf16[7,256,2048]{2,1,0:T(8,128)(2,1)S(1)}, bf16[7,256,2048]{2,1,0:T(8,128)(2,1)}, u32[]{:S(2)}) %copy-start.3) | copy-done | bytes 7340056
  60.1 11.8 %weight.3 = (bf16[896,14336]{1,0:T(8,128)(2,1)}, f32[1,14336]{1,0:T(1,128)}) custom-call(bf16[896,256]{1,0:T(8,128)(2,1)S(1)} %get-tuple-element.12.saved_t, bf16[7,256,2048]{2,1,0:T(8,128)(2,1)S(1)} %copy-done.3, f32[1,14336]{1,0:T(1,128)S(1)} %get-tuple-element.14.bias), custom_call_target="tpu_custom_call" | custom-call | flops 6576668672 | bytes 33030144 | tf_op jit(solution)/shard_map/weight/pallas_call | solution.py:294
  71.9 0.0 collective-permute-done
  71.9 0.7 %add_convert_fusion = bf16[128,896]{1,0:T(8,128)(2,1)} fusion(bf16[128,896]{1,0:T(8,128)(2,1)S(1)} %collective-permute-done, bf16[128,896]{1,0:T(8,128)(2,1)S(1)} %get-tuple-element.10), kind=kLoop, calls=%fused_computation | loop fusion | flops 458752 | bytes 688128 | tf_op jit(solution)/shard_map/convert_element_type | solution.py:318
Async XLA Ops:
  1.4 1.0 %copy-start = (bf16[16,14336]{1,0:T(8,128)(2,1)S(1)}, bf16[16,14336]{1,0:T(8,128)(2,1)}, u32[]{:S(2)}) copy-start(bf16[16,14336]{1,0:T(8,128)(2,1)} %values.1) | copy-start | bytes 1376260
  2.5 0.9 %copy-start.1 = (bf16[128,896]{1,0:T(8,128)(2,1)S(1)}, bf16[128,896]{1,0:T(8,128)(2,1)}, u32[]{:S(2)}) copy-start(bf16[128,896]{1,0:T(8,128)(2,1)} %saved.1) | copy-start | bytes 688132
  3.4 0.7 copy-start.2
  55.3 16.6 %collective-permute-start = (bf16[128,896]{1,0:T(8,128)(2,1)S(1)}, bf16[128,896]{1,0:T(8,128)(2,1)S(1)}, u32[]{:S(2)}, u32[]{:S(2)}) collective-permute-start(bf16[128,896]{1,0:T(8,128)(2,1)S(1)} %get-tuple-element.11), channel_id=1, source_target_pairs={{0,1},{1,0},{2,3},{3,2},{4,5},{5,4},{6,7},{7,6},{8,9},{9,8},{10,11... | collective-permute-start | bytes 688136 | tf_op jit(solution)/shard_map/ppermute | solution.py:293
  57.0 3.1 %copy-start.3 = (bf16[7,256,2048]{2,1,0:T(8,128)(2,1)S(1)}, bf16[7,256,2048]{2,1,0:T(8,128)(2,1)}, u32[]{:S(2)}) copy-start(bf16[7,256,2048]{2,1,0:T(8,128)(2,1)} %get-tuple-element.13.hid) | copy-start | bytes 22020100
